TPU v7x, 32 devices: a whole 2x2x4 slice. The times are simulated.
32 devices in a mesh: groups: 2 (over y), row: 4 (over z), col: 4 (over x, core).
Axes of the slice: x: 2, y: 2, z: 4, core: 2. Of those that a mesh axis runs over, the one named last changes fastest.
Arguments:
- grad_users: bfloat16 [32768, 128], P(('groups', 'row', 'col')), parts along dimension 0, may hold values from -6 to 6
- grad_items: bfloat16 [16384, 128], P(('groups', 'col', 'row')), parts along dimension 0, may hold values from -6 to 6
- user_degree: int32 [32768], P(('groups', 'row', 'col')), parts along dimension 0, may hold values from 1 to 4
- item_degree: int32 [16384], P(('groups', 'col', 'row')), parts along dimension 0, may hold values from 1 to 4
- tile_values: bfloat16 [768, 256, 256], P(('groups', 'row', 'col')), parts along dimension 0, may hold values from -0.109375 to 0.109375
- tile_row: int32 [768], P(('groups', 'row', 'col')), parts along dimension 0, may hold values from 0 to 15, as said below
- tile_col: int32 [768], P(('groups', 'row', 'col')), parts along dimension 0, may hold values from 0 to 7, as said below
Outputs:
- user_grad: bfloat16 [32768, 128], P(('groups', 'row', 'col')), parts along dimension 0
- item_grad: bfloat16 [16384, 128], P(('groups', 'col', 'row')), parts along dimension 0
There are 2 independent parts, one for each index of `groups`. A program takes and returns all parts, laid end to end along the dimension named above; each array names one. Nothing has to cross between parts.
Inputs may be any that keep to these rules, and one draw needn't show every extreme that they name: tile_row counts user blocks inside the row range of the owning device (slot s // 24 = r * 4 + c owns row range r); the 24 tiles of one owner stand at distinct (tile_row, tile_col) positions. tile_col counts item blocks inside the column range c of the owning device.
All inputs are finite; a program needn't handle non-finite values.
Results may differ from a plain program's by a relative error of at most 0.0075.
Values may be sent and summed in bfloat16 or wider, within the bound.
A program may use at most 64 MiB of HBM per device.

v0:
```python
import jax
import jax.numpy as jnp
from jax import lax
from jax.sharding import PartitionSpec as P

LAYERS = 2


def shards(grad_users, grad_items, user_degree, item_degree, tile_values, tile_row, tile_col):
    tile_size = tile_values.shape[1]
    width = grad_users.shape[1]
    user_blocks = grad_users.shape[0] * lax.axis_size("col") // tile_size
    item_rows = grad_items.shape[0]
    item_blocks = item_rows * lax.axis_size("row") // tile_size
    weight_per_layer = 1.0 / (LAYERS + 1)
    user_scale = lax.rsqrt(user_degree.astype(jnp.float32))[:, None]
    user_base = weight_per_layer * grad_users.astype(jnp.float32)
    row_onehot = (tile_row[None, :] == jnp.arange(user_blocks, dtype=jnp.int32)[:, None]).astype(
        jnp.float32
    )
    column_indicator = (
        tile_col[None, :] == jnp.arange(item_blocks, dtype=jnp.int32)[:, None]
    ).astype(jnp.float32)
    users_now = user_base.astype(jnp.bfloat16)
    item_scale = lax.rsqrt(item_degree.astype(jnp.float32))[:, None]
    item_base = weight_per_layer * grad_items.astype(jnp.float32)
    items_now = item_base.astype(jnp.bfloat16)
    for layer_position in range(LAYERS):
        scaled_items = (item_scale * items_now.astype(jnp.float32)).astype(jnp.bfloat16)
        blocks = lax.all_gather(scaled_items, "row", axis=0, tiled=True).reshape(
            item_blocks, tile_size, width
        )
        users_picked = blocks[tile_col]
        users_matrix_product = jnp.einsum(
            "nab,nbd->nad", tile_values, users_picked, preferred_element_type=jnp.float32
        )
        users_partial_value = jnp.einsum(
            "un,nad->uad", row_onehot, users_matrix_product, precision=lax.Precision.HIGHEST
        )
        user_sum = lax.psum_scatter(
            users_partial_value.reshape(user_blocks * tile_size, width).astype(jnp.bfloat16),
            "col",
            scatter_dimension=0,
            tiled=True,
        ).astype(jnp.float32)
        scaled = (user_scale * users_now.astype(jnp.float32)).astype(jnp.bfloat16)
        whole = lax.all_gather(scaled, "col", axis=0, tiled=True).reshape(
            user_blocks, tile_size, width
        )
        picked = whole[tile_row]
        matrix_product = jnp.einsum(
            "nba,nbd->nad", tile_values, picked, preferred_element_type=jnp.float32
        )
        partial_value = jnp.einsum(
            "rg,gcj->rcj", column_indicator, matrix_product, precision=lax.Precision.HIGHEST
        )
        item_sum = lax.psum_scatter(
            partial_value.reshape(item_blocks * tile_size, width),
            "row",
            scatter_dimension=0,
            tiled=True,
        )
        users_now = (user_base + user_scale * user_sum).astype(jnp.bfloat16)
        items_now = (item_base + item_scale * item_sum).astype(jnp.bfloat16)
    return (users_now, items_now)


def solution(mesh):
    return jax.shard_map(
        shards,
        mesh=mesh,
        in_specs=(
            P(("groups", "row", "col"), None),
            P(("groups", "col", "row"), None),
            P(("groups", "row", "col")),
            P(("groups", "col", "row")),
            P(("groups", "row", "col"), None, None),
            P(("groups", "row", "col")),
            P(("groups", "row", "col")),
        ),
        out_specs=(P(("groups", "row", "col"), None), P(("groups", "col", "row"), None)),
        check_vma=False,
    )
```

profile of v0, /device:TPU:0, one launch (start us, length us, event | category | flops | bytes accessed | tf_op | source)
XLA Modules:
  0.0 229.2 jit_solution(10514154936415127606)
XLA Ops:
  10.7 18.9 %all-gather.3.cloned.1.call-done = bf16[4096,128]{1,0:T(8,128)(2,1)} async-done(((bf16[1024,128]{1,0:T(8,128)(2,1)}), bf16[4096,128]{1,0:T(8,128)(2,1)}) %all-gather.3.cloned.1.call-update) | async-done | bytes 1048592 | tf_op jit(solution)/shard_map/all_gather | solution.py:47
  29.6 3.2 %gather_fusion = bf16[24,256,128]{2,1,0:T(8,128)(2,1)} fusion(bf16[16,256,128]{2,1,0:T(8,128)(2,1)} %bitcast.46, s32[1024]{0:T(1024)S(1)} %pad_clamp_fusion.1), kind=kCustom, calls=%fused_computation | custom fusion | bytes 3145824 | tf_op jit(solution)/shard_map/gather | solution.py:50
  32.8 3.7 %fusion.26 = f32[24,128,256]{2,1,0:T(8,128)} fusion(bf16[24,256,128]{2,1,0:T(8,128)(2,1)} %gather_fusion, bf16[24,256,256]{2,1,0:T(8,128)(2,1)S(1)} %copy-done), kind=kOutput, calls=%fused_computation.40 | convolution fusion | flops 402653184 | bytes 7864320 | tf_op jit(solution)/shard_map/nba,nbd->nad/dot_general | solution.py:51
  36.5 3.6 %copy.13 = f32[24,128,256]{1,0,2:T(8,128)} copy(f32[24,128,256]{2,1,0:T(8,128)} %fusion.26) | data formatting | bytes 6291456 | tf_op jit(solution)/shard_map/nba,nbd->nad/dot_general | solution.py:51
  40.1 3.1 %fusion.6 = f32[8,256,128]{2,0,1:T(8,128)S(1)} fusion(f32[24,128,256]{1,0,2:T(8,128)} %copy.13, s32[24]{0:T(128)S(1)} %copy-done.4), kind=kOutput, calls=%fused_computation.10 | convolution fusion | flops 75497664 | bytes 4194400 | tf_op jit(solution)/shard_map/rg,gcj->rcj/dot_general | solution.py:54
  44.5 27.2 %reduce-scatter.5.cloned.1.call-done = f32[512,128]{1,0:T(8,128)} async-done(((f32[2048,128]{1,0:T(8,128)}), f32[512,128]{1,0:T(8,128)}) %reduce-scatter.5.cloned.1.call-update) | async-done | bytes 262160 | tf_op jit(solution)/shard_map/reduce_scatter | solution.py:57
  72.8 16.4 %all_gather.13 = bf16[2048,128]{1,0:T(8,128)(2,1)} all-gather(bf16[512,128]{1,0:T(8,128)(2,1)S(1)} %get-tuple-element.5), channel_id=1, replica_groups=mesh['groups'=2,'row'=4,'col'=4] {'row'}, dimensions={0}, use_global_device_ids=true | all-gather | bytes 655360 | tf_op jit(solution)/shard_map/all_gather | solution.py:30
  89.2 3.0 %gather_fusion.1 = bf16[24,256,128]{2,1,0:T(8,128)(2,1)} fusion(bf16[8,256,128]{2,1,0:T(8,128)(2,1)} %bitcast.41, s32[1024]{0:T(1024)S(1)} %pad_clamp_fusion), kind=kCustom, calls=%fused_computation.1 | custom fusion | bytes 3145824 | tf_op jit(solution)/shard_map/gather | solution.py:33
  92.2 4.2 %fusion.27 = f32[24,128,256]{2,1,0:T(8,128)} fusion(bf16[24,256,128]{2,1,0:T(8,128)(2,1)} %gather_fusion.1, bf16[24,256,256]{2,1,0:T(8,128)(2,1)S(1)} %copy-done), kind=kOutput, calls=%fused_computation.41 | convolution fusion | flops 402653184 | bytes 7864320 | tf_op jit(solution)/shard_map/nab,nbd->nad/dot_general | solution.py:34
  96.5 3.6 %copy.14 = f32[24,128,256]{1,0,2:T(8,128)} copy(f32[24,128,256]{2,1,0:T(8,128)} %fusion.27) | data formatting | bytes 6291456 | tf_op jit(solution)/shard_map/nab,nbd->nad/dot_general | solution.py:34
  100.0 3.2 %fusion.8 = bf16[16,256,128]{2,0,1:T(8,128)(2,1)S(1)} fusion(f32[24,128,256]{1,0,2:T(8,128)} %copy.14, s32[24]{0:T(128)S(1)} %copy-done.3), kind=kOutput, calls=%fused_computation.12 | convolution fusion | flops 151519616 | bytes 4194400 | tf_op jit(solution)/shard_map/un,nad->uad/dot_general | solution.py:37
  104.6 15.5 %all_gather.14 = bf16[2048,128]{1,0:T(8,128)(2,1)} all-gather(bf16[512,128]{1,0:T(8,128)(2,1)S(1)} %get-tuple-element.4), channel_id=1, replica_groups=mesh['groups'=2,'row'=4,'col'=4] {'row'}, dimensions={0}, use_global_device_ids=true | all-gather | bytes 655360 | tf_op jit(solution)/shard_map/all_gather | solution.py:30
  120.1 3.0 %gather_fusion.2 = bf16[24,256,128]{2,1,0:T(8,128)(2,1)} fusion(bf16[8,256,128]{2,1,0:T(8,128)(2,1)} %bitcast.40, s32[1024]{0:T(1024)S(1)} %pad_clamp_fusion), kind=kCustom, calls=%fused_computation.2 | custom fusion | bytes 3145824 | tf_op jit(solution)/shard_map/gather | solution.py:33
  123.1 4.2 %fusion.28 = f32[24,128,256]{2,1,0:T(8,128)} fusion(bf16[24,256,128]{2,1,0:T(8,128)(2,1)} %gather_fusion.2, bf16[24,256,256]{2,1,0:T(8,128)(2,1)S(1)} %copy-done), kind=kOutput, calls=%fused_computation.42 | convolution fusion | flops 402653184 | bytes 7864320 | tf_op jit(solution)/shard_map/nab,nbd->nad/dot_general | solution.py:34
  127.4 3.6 %copy.15 = f32[24,128,256]{1,0,2:T(8,128)} copy(f32[24,128,256]{2,1,0:T(8,128)} %fusion.28) | data formatting | bytes 6291456 | tf_op jit(solution)/shard_map/nab,nbd->nad/dot_general | solution.py:34
  131.0 3.3 %fusion.11 = bf16[16,256,128]{2,0,1:T(8,128)(2,1)S(1)} fusion(f32[24,128,256]{1,0,2:T(8,128)} %copy.15, s32[24]{0:T(128)S(1)} %copy-done.3), kind=kOutput, calls=%fused_computation.13 | convolution fusion | flops 151519616 | bytes 4194400 | tf_op jit(solution)/shard_map/un,nad->uad/dot_general | solution.py:37
  135.6 24.0 %reduce-scatter.9.cloned.1.call-done = bf16[1024,128]{1,0:T(8,128)(2,1)} async-done(((bf16[4096,128]{1,0:T(8,128)(2,1)}), bf16[1024,128]{1,0:T(8,128)(2,1)}) %reduce-scatter.9.cloned.1.call-update) | async-done | bytes 262160 | tf_op jit(solution)/shard_map/reduce_scatter | solution.py:40
  159.5 2.1 multiply_convert_fusion
  161.9 16.7 %all-gather.5.cloned.1.call-done = bf16[4096,128]{1,0:T(8,128)(2,1)} async-done(((bf16[1024,128]{1,0:T(8,128)(2,1)}), bf16[4096,128]{1,0:T(8,128)(2,1)}) %all-gather.5.cloned.1.call-update) | async-done | bytes 1048592 | tf_op jit(solution)/shard_map/all_gather | solution.py:47
  178.5 3.2 %gather_fusion.3 = bf16[24,256,128]{2,1,0:T(8,128)(2,1)} fusion(bf16[16,256,128]{2,1,0:T(8,128)(2,1)} %bitcast.47, s32[1024]{0:T(1024)S(1)} %pad_clamp_fusion.1), kind=kCustom, calls=%fused_computation.3 | custom fusion | bytes 3145824 | tf_op jit(solution)/shard_map/gather | solution.py:50
  181.7 3.7 %fusion.29 = f32[24,128,256]{2,1,0:T(8,128)} fusion(bf16[24,256,128]{2,1,0:T(8,128)(2,1)} %gather_fusion.3, bf16[24,256,256]{2,1,0:T(8,128)(2,1)S(1)} %copy-done), kind=kOutput, calls=%fused_computation.43 | convolution fusion | flops 402653184 | bytes 7864320 | tf_op jit(solution)/shard_map/nba,nbd->nad/dot_general | solution.py:51
  185.4 3.6 %copy.16 = f32[24,128,256]{1,0,2:T(8,128)} copy(f32[24,128,256]{2,1,0:T(8,128)} %fusion.29) | data formatting | bytes 6291456 | tf_op jit(solution)/shard_map/nba,nbd->nad/dot_general | solution.py:51
  189.0 3.1 %fusion = f32[8,256,128]{2,0,1:T(8,128)S(1)} fusion(f32[24,128,256]{1,0,2:T(8,128)} %copy.16, s32[24]{0:T(128)S(1)} %copy-done.5), kind=kOutput, calls=%fused_computation.4 | convolution fusion | flops 75497664 | bytes 4194400 | tf_op jit(solution)/shard_map/rg,gcj->rcj/dot_general | solution.py:54
  193.3 27.3 %reduce-scatter.11.cloned.1.call-done = f32[512,128]{1,0:T(8,128)} async-done(((f32[2048,128]{1,0:T(8,128)}), f32[512,128]{1,0:T(8,128)}) %reduce-scatter.11.cloned.1.call-update) | async-done | bytes 262160 | tf_op jit(solution)/shard_map/reduce_scatter | solution.py:57
  (40 shorter events, 11.7 us)
Async XLA Ops:
  7.2 25.6 %copy-start = (bf16[24,256,256]{2,1,0:T(8,128)(2,1)S(1)}, bf16[24,256,256]{2,1,0:T(8,128)(2,1)}, u32[]{:S(2)}) copy-start(bf16[24,256,256]{2,1,0:T(8,128)(2,1)} %param.11) | copy-start | bytes 9437188
  7.2 22.4 %all-gather.3.cloned.1.call-start = ((), (), s32[]{:S(2)}) async-start(), calls=%async_computation.4 | async-start | bytes 1310720 | tf_op jit(solution)/shard_map/all_gather | solution.py:47
  10.0 61.7 %reduce-scatter.5.cloned.1.call-start = ((), (), s32[]{:S(2)}) async-start(), calls=%async_computation.5 | async-start | bytes 1310720 | tf_op jit(solution)/shard_map/reduce_scatter | solution.py:57
  36.5 3.6 %copy-start.4 = (s32[24]{0:T(128)S(1)}, s32[24]{0:T(128)}, u32[]{:S(2)}) copy-start(s32[24]{0:T(128)} %param.13) | copy-start | bytes 292
  40.1 4.4 %copy-start.6 = (s32[512]{0:T(512)S(1)}, s32[512]{0:T(512)}, u32[]{:S(2)}) copy-start(s32[512]{0:T(512)} %param.10) | copy-start | bytes 6148
  40.1 31.6 %copy-start.2 = (bf16[512,128]{1,0:T(8,128)(2,1)S(1)}, bf16[512,128]{1,0:T(8,128)(2,1)}, u32[]{:S(2)}) copy-start(bf16[512,128]{1,0:T(8,128)(2,1)} %param.8) | copy-start | bytes 393220
  44.4 91.1 %reduce-scatter.7.cloned.1.call-start = ((), (), s32[]{:S(2)}) async-start(), calls=%async_computation.6 | async-start | bytes 1310720 | tf_op jit(solution)/shard_map/reduce_scatter | solution.py:40
  96.5 3.6 %copy-start.3 = (s32[24]{0:T(128)S(1)}, s32[24]{0:T(128)}, u32[]{:S(2)}) copy-start(s32[24]{0:T(128)} %param.12) | copy-start | bytes 292
  104.6 55.0 %reduce-scatter.9.cloned.1.call-start = ((), (), s32[]{:S(2)}) async-start(), calls=%async_computation.7 | async-start | bytes 1310720 | tf_op jit(solution)/shard_map/reduce_scatter | solution.py:40
  130.9 28.6 %copy-start.1 = (bf16[1024,128]{1,0:T(8,128)(2,1)S(1)}, bf16[1024,128]{1,0:T(8,128)(2,1)}, u32[]{:S(2)}) copy-start(bf16[1024,128]{1,0:T(8,128)(2,1)} %param.7) | copy-start | bytes 786436
  135.5 43.0 %all-gather.5.cloned.1.call-start = ((), (), s32[]{:S(2)}) async-start(), calls=%async_computation.8 | async-start | bytes 1310720 | tf_op jit(solution)/shard_map/all_gather | solution.py:47
  161.6 59.0 %reduce-scatter.11.cloned.1.call-start = ((), (), s32[]{:S(2)}) async-start(), calls=%async_computation.9 | async-start | bytes 1310720 | tf_op jit(solution)/shard_map/reduce_scatter | solution.py:57
  185.4 3.6 %copy-start.5 = (s32[24]{0:T(128)S(1)}, s32[24]{0:T(128)}, u32[]{:S(2)}) copy-start(s32[24]{0:T(128)} %param.13) | copy-start | bytes 292
Sparse Core Ops, SparseCore 0:
  10.1 19.4 all-gather.2
  44.6 27.1 reduce-scatter.4
  104.7 23.2 reduce-scatter.6
  135.6 23.8 reduce-scatter.8
  161.8 16.7 all-gather.4
  193.4 27.1 reduce-scatter.10
where the time goes:
time: 230 us; the launch traced here: 229 us
  waiting for transfers between devices  114 us (50%)
  blocking collectives  32 us (14%)
  local copies, waits for them, and re-layouts  31.5 us (14%)
  matrix products  28.7 us (12%)
  between operations  14.2 us (6%)
  other arithmetic  8.33 us (4%)
    reduce_scatter x2, waiting for transfers between devices, shards(): lax.psum_scatter(partial_value.reshape(item_blocks * tile_size, width), '...  54.5 us
    all_gather x2, waiting for transfers between devices, shards(): lax.all_gather(scaled, 'col', axis=0, tiled=True)  35.5 us
    all_gather x2, blocking collectives, shards(): lax.all_gather(scaled_items, 'row', axis=0, tiled=True)  32 us
    reduce_scatter x2, waiting for transfers between devices, shards(): lax.psum_scatter(users_partial_value.reshape(user_blocks * tile_size, wid...  24 us
    dot_general x2, matrix products, shards(): jnp.einsum('nab,nbd->nad', tile_values, users_picked, preferred_element_t...  8.46 us
    dot_general x2, matrix products, shards(): jnp.einsum('nba,nbd->nad', tile_values, picked, preferred_element_type=jn...  7.47 us
    dot_general x2, local copies, waits for them, and re-layouts, shards(): jnp.einsum('nab,nbd->nad', tile_values, users_picked, preferred_element_t...  7.15 us
    dot_general x2, local copies, waits for them, and re-layouts, shards(): jnp.einsum('nba,nbd->nad', tile_values, picked, preferred_element_type=jn...  7.14 us
  transfers between devices with their start and end apart: 6, of which 5 were waited for; matrix products, arithmetic and copies ran while one was open for 7% of the time, Pallas kernels for 0%

commit v1 on v0

v1 whole, which is shorter than its diff:
```python
import functools

import jax
import jax.numpy as jnp
from jax import lax
from jax.experimental import pallas as pl
from jax.experimental.pallas import tpu as pltpu
from jax.sharding import PartitionSpec as P

LAYERS = 2
MESH = pl.DeviceIdType.MESH
WEIGHT = 1.0 / (LAYERS + 1)


def kernel(
    n_row, n_col, n_tiles, tile, width, u_rows, i_rows,
    idx, gu, gi, su, si, tiles_hbm,
    out_u, out_i,
    users_0, users_1, items_0, items_1, up_out, up_in, ip_out, ip_in, sum_u, sum_i, tiles, tiles_t,
    u_send, u_recv, i_send, i_recv, tile_sem,
):
    mr, mc = lax.axis_index("row"), lax.axis_index("col")
    u_blocks = u_rows * n_col // tile
    i_blocks = i_rows * n_row // tile
    at_row, at_col = 0, n_tiles
    at_prev_row, at_prev_col = 2 * n_tiles, 3 * n_tiles
    at_last_row, at_last_col = 4 * n_tiles, 4 * n_tiles + u_blocks

    barrier = pltpu.get_barrier_semaphore()

    def greet(axis, me, n):
        def body(d, carry):
            pl.semaphore_signal(
                barrier, inc=1, device_id={axis: lax.rem(me + d, n)}, device_id_type=MESH
            )
            return carry

        lax.fori_loop(1, n, body, 0)

    greet("row", mr, n_row)
    greet("col", mc, n_col)
    tile_copy = pltpu.make_async_copy(tiles_hbm, tiles, tile_sem)
    tile_copy.start()

    users_all, items_all = (users_0, users_1), (items_0, items_1)

    def part(ref, p, rows):
        if rows % tile == 0:
            k = rows // tile
            return ref.at[pl.ds(p * k, k)]
        per = tile // rows
        return ref.at[lax.div(p, per), pl.ds(pl.multiple_of(lax.rem(p, per) * rows, rows), rows)]

    def slot(ref, l, d, rows):
        return ref.at[l, d] if rows % tile == 0 else ref.at[l, d, 0]

    def gather_items(l, d):
        return pltpu.make_async_remote_copy(
            src_ref=part(items_all[l], mr, i_rows),
            dst_ref=part(items_all[l], mr, i_rows),
            send_sem=i_send.at[l, 0, d],
            recv_sem=i_recv.at[l, 0, d],
            device_id={"row": lax.rem(mr + d, n_row)},
            device_id_type=MESH,
        )

    def gather_users(l, d):
        return pltpu.make_async_remote_copy(
            src_ref=part(users_all[l], mc, u_rows),
            dst_ref=part(users_all[l], mc, u_rows),
            send_sem=u_send.at[l, 0, d],
            recv_sem=u_recv.at[l, 0, d],
            device_id={"col": lax.rem(mc + d, n_col)},
            device_id_type=MESH,
        )

    def scatter_items(l, d):
        peer = lax.rem(mr + d, n_row)
        return pltpu.make_async_remote_copy(
            src_ref=part(ip_out.at[l], peer, i_rows),
            dst_ref=slot(ip_in, l, d, i_rows),
            send_sem=i_send.at[l, 1, d],
            recv_sem=i_recv.at[l, 1, d],
            device_id={"row": peer},
            device_id_type=MESH,
        )

    def scatter_users(l, d):
        peer = lax.rem(mc + d, n_col)
        return pltpu.make_async_remote_copy(
            src_ref=part(up_out.at[l], peer, u_rows),
            dst_ref=slot(up_in, l, d, u_rows),
            send_sem=u_send.at[l, 1, d],
            recv_sem=u_recv.at[l, 1, d],
            device_id={"col": peer},
            device_id_type=MESH,
        )

    def each(copies, l, n, act):
        def body(d, carry):
            act(copies(l, d))
            return carry

        lax.fori_loop(1, n, body, 0)

    start = lambda c: c.start()
    wait_recv = lambda c: c.wait_recv()
    wait_send = lambda c: c.wait_send()

    def begin(rows, own, grad, scale, gathered):
        chunk = min(rows, 128)

        def body(k, carry):
            here = pl.ds(pl.multiple_of(k * chunk, chunk), chunk)
            now = (WEIGHT * grad[here, :].astype(jnp.float32)).astype(jnp.bfloat16)
            at = own + k * chunk
            mine = pl.ds(pl.multiple_of(lax.rem(at, tile), chunk), chunk)
            gathered[0][lax.div(at, tile), mine, :] = (
                scale[here, :] * now.astype(jnp.float32)
            ).astype(jnp.bfloat16)
            return carry

        lax.fori_loop(0, rows // chunk, body, 0)

    begin(i_rows, mr * i_rows, gi, si, items_all)
    begin(u_rows, mc * u_rows, gu, su, users_all)
    pl.semaphore_wait(barrier, n_row + n_col - 2)
    each(gather_items, 0, n_row, start)
    each(gather_users, 0, n_col, start)

    sum_u[0] = jnp.zeros((tile, width), jnp.float32)
    sum_i[0] = jnp.zeros((tile, width), jnp.float32)
    tile_copy.wait()

    def turn(n, carry):
        tiles_t[n] = tiles[n].T
        return carry

    lax.fori_loop(0, n_tiles, turn, 0)

    group = 4 if n_tiles % 4 == 0 else 1

    def products(l, mats, blocks, sums, at_block, at_prev):
        def body(g, carry):
            parts = []
            for k in range(group):
                n = g * group + k
                b = idx[at_block + n]
                parts.append(jnp.dot(mats[n], blocks[l][b], preferred_element_type=jnp.float32))
            for k in range(group):
                n = g * group + k
                sums[n + 1] = parts[k] + sums[idx[at_prev + n]]
            return carry

        lax.fori_loop(0, n_tiles // group, body, 0)

    def stage(l, out, sums, at_last, blocks):
        def body(b, carry):
            out[l, b] = sums[idx[at_last + b]].astype(jnp.bfloat16)
            return carry

        lax.fori_loop(0, blocks, body, 0)

    def update(l, n, rows, own, grad, scale, out, inn, result, gathered):
        chunk = min(rows, 128)

        def body(k, carry):
            here = pl.ds(pl.multiple_of(k * chunk, chunk), chunk)
            at = own + k * chunk
            block = lax.div(at, tile)
            mine = pl.ds(pl.multiple_of(lax.rem(at, tile), chunk), chunk)
            total = out[l, block, mine, :].astype(jnp.float32)
            sub = min(rows, tile)
            sub_at = pl.ds(pl.multiple_of(lax.rem(k * chunk, sub), chunk), chunk)

            def add(d, total):
                return total + inn[l, d, lax.div(k * chunk, sub), sub_at, :].astype(jnp.float32)

            if n <= 8:
                for d in range(1, n):
                    total = add(d, total)
            else:
                total = lax.fori_loop(1, n, add, total)
            factor = scale[here, :]
            now = (WEIGHT * grad[here, :].astype(jnp.float32) + factor * total).astype(jnp.bfloat16)
            if l + 1 < LAYERS:
                gathered[l + 1][block, mine, :] = (factor * now.astype(jnp.float32)).astype(jnp.bfloat16)
            else:
                result[here, :] = now
            return carry

        lax.fori_loop(0, rows // chunk, body, 0)

    for l in range(LAYERS):
        each(gather_users, l, n_col, wait_recv)
        products(l, tiles_t, users_all, sum_i, at_row, at_prev_col)
        stage(l, ip_out, sum_i, at_last_col, i_blocks)
        each(scatter_items, l, n_row, start)
        each(gather_items, l, n_row, wait_recv)
        products(l, tiles, items_all, sum_u, at_col, at_prev_row)
        stage(l, up_out, sum_u, at_last_row, u_blocks)
        each(scatter_users, l, n_col, start)
        each(scatter_items, l, n_row, wait_recv)
        update(l, n_row, i_rows, mr * i_rows, gi, si, ip_out, ip_in, out_i, items_all)
        if l + 1 < LAYERS:
            each(gather_items, l + 1, n_row, start)
        each(scatter_users, l, n_col, wait_recv)
        update(l, n_col, u_rows, mc * u_rows, gu, su, up_out, up_in, out_u, users_all)
        if l + 1 < LAYERS:
            each(gather_users, l + 1, n_col, start)
    for l in range(LAYERS):
        each(gather_items, l, n_row, wait_send)
        each(gather_users, l, n_col, wait_send)
        each(scatter_items, l, n_row, wait_send)
        each(scatter_users, l, n_col, wait_send)


def shards(grad_users, grad_items, user_degree, item_degree, tile_values, tile_row, tile_col):
    n_row, n_col = lax.axis_size("row"), lax.axis_size("col")
    n_tiles, tile = tile_values.shape[:2]
    u_rows, width = grad_users.shape
    i_rows = grad_items.shape[0]
    u_blocks, i_blocks = u_rows * n_col // tile, i_rows * n_row // tile
    su = jnp.broadcast_to(lax.rsqrt(user_degree.astype(jnp.float32))[:, None], (u_rows, width))
    si = jnp.broadcast_to(lax.rsqrt(item_degree.astype(jnp.float32))[:, None], (i_rows, width))
    slot = jnp.arange(n_tiles, dtype=jnp.int32)

    def latest(keys, wanted, before):
        hit = (keys[None, :] == wanted[:, None]) & (slot[None, :] < before[:, None])
        return jnp.max(jnp.where(hit, slot[None, :] + 1, 0), axis=1)

    idx = jnp.concatenate(
        [
            tile_row,
            tile_col,
            latest(tile_row, tile_row, slot),
            latest(tile_col, tile_col, slot),
            latest(tile_row, jnp.arange(u_blocks, dtype=jnp.int32), jnp.full(u_blocks, n_tiles)),
            latest(tile_col, jnp.arange(i_blocks, dtype=jnp.int32), jnp.full(i_blocks, n_tiles)),
        ]
    )
    u_sub, i_sub = min(u_rows, tile), min(i_rows, tile)
    vmem = pl.BlockSpec(memory_space=pltpu.VMEM)
    bf16, f32 = jnp.bfloat16, jnp.float32
    return pl.pallas_call(
        functools.partial(kernel, n_row, n_col, n_tiles, tile, width, u_rows, i_rows),
        out_shape=(
            jax.ShapeDtypeStruct((u_rows, width), bf16),
            jax.ShapeDtypeStruct((i_rows, width), bf16),
        ),
        in_specs=[pl.BlockSpec(memory_space=pltpu.SMEM), vmem, vmem, vmem, vmem,
                  pl.BlockSpec(memory_space=pl.ANY)],
        out_specs=(vmem, vmem),
        scratch_shapes=[
            pltpu.VMEM((u_blocks, tile, width), bf16),
            pltpu.VMEM((u_blocks, tile, width), bf16),
            pltpu.VMEM((i_blocks, tile, width), bf16),
            pltpu.VMEM((i_blocks, tile, width), bf16),
            pltpu.VMEM((LAYERS, u_blocks, tile, width), bf16),
            pltpu.VMEM((LAYERS, n_col, u_rows // u_sub, u_sub, width), bf16),
            pltpu.VMEM((LAYERS, i_blocks, tile, width), bf16),
            pltpu.VMEM((LAYERS, n_row, i_rows // i_sub, i_sub, width), bf16),
            pltpu.VMEM((n_tiles + 1, tile, width), f32),
            pltpu.VMEM((n_tiles + 1, tile, width), f32),
            pltpu.VMEM((n_tiles, tile, tile), bf16),
            pltpu.VMEM((n_tiles, tile, tile), bf16),
            pltpu.SemaphoreType.DMA((LAYERS, 2, n_col)),
            pltpu.SemaphoreType.DMA((LAYERS, 2, n_col)),
            pltpu.SemaphoreType.DMA((LAYERS, 2, n_row)),
            pltpu.SemaphoreType.DMA((LAYERS, 2, n_row)),
            pltpu.SemaphoreType.DMA,
        ],
        compiler_params=pltpu.CompilerParams(
            collective_id=0, has_side_effects=True, vmem_limit_bytes=40 * 1024 * 1024
        ),
    )(idx, grad_users, grad_items, su, si, tile_values)


def solution(mesh):
    return jax.shard_map(
        shards,
        mesh=mesh,
        in_specs=(
            P(("groups", "row", "col"), None),
            P(("groups", "col", "row"), None),
            P(("groups", "row", "col")),
            P(("groups", "col", "row")),
            P(("groups", "row", "col"), None, None),
            P(("groups", "row", "col")),
            P(("groups", "row", "col")),
        ),
        out_specs=(P(("groups", "row", "col"), None), P(("groups", "col", "row"), None)),
        check_vma=False,
    )
```

time: 230 us -> 71.7 us (0.31)
  the two profiles are of different devices: /device:TPU:0 before, /device:TPU:9 now
where the time goes in v1:
time: 71.7 us; the launch traced here: 71.4 us
  Pallas kernels  60.7 us (85%)
  local copies, waits for them, and re-layouts  6.17 us (9%)
  other arithmetic  3.86 us (5%)
    pallas_call x1, Pallas kernels, shards(): pl.pallas_call(functools.partial(kernel, n_row, n_col, n_tiles, tile, wid...  60.7 us
    unnamed x8, local copies, waits for them, and re-layouts  5.1 us
    reduce_max x3, other arithmetic, latest(): return jnp.max(jnp.where(hit, slot[None, :] + 1, 0), axis=1)  2.47 us

profile of v1, /device:TPU:9, one launch (start us, length us, event | category | flops | bytes accessed | tf_op | source)
XLA Modules:
  0.0 71.4 jit_solution(15908880701212996050)
XLA Ops:
  0.7 0.8 %select_reduce_fusion.3 = s32[8]{0:T(128)S(1)} fusion(s32[24]{0:T(128)S(1)} %iota_add_fusion, s32[24]{0:T(128)} %param.13, pred[24]{0:T(512)(128)(4,1)S(1)} %iota_compare_fusion.3), kind=kLoop, calls=%fused_computation.9 | loop fusion | flops 760 | bytes 248 | tf_op jit(solution)/shard_map/reduce_max | solution.py:230
  1.4 0.8 %select_reduce_fusion.2 = s32[16]{0:T(128)S(1)} fusion(s32[24]{0:T(128)S(1)} %iota_add_fusion, s32[24]{0:T(128)} %param.12, pred[24]{0:T(512)(128)(4,1)S(1)} %iota_compare_fusion.3), kind=kLoop, calls=%fused_computation.5 | loop fusion | flops 1520 | bytes 280 | tf_op jit(solution)/shard_map/reduce_max | solution.py:230
  2.2 0.9 %select_reduce_fusion = (s32[24]{0:T(128)S(1)}, s32[24]{0:T(128)S(1)}) fusion(s32[24]{0:T(128)} %param.13, s32[24]{0:T(128)S(1)} %iota_add_fusion, s32[24]{0:T(128)} %param.12), kind=kLoop, calls=%fused_computation | loop fusion | flops 5136 | bytes 480 | tf_op jit(solution)/shard_map/reduce_max | solution.py:230
  3.1 0.8 %concatenate.3.idx = s32[120]{0:T(128)S(1)} concatenate(s32[24]{0:T(128)} %param.12, s32[24]{0:T(128)} %param.13, s32[24]{0:T(128)S(1)} %get-tuple-element.3, s32[24]{0:T(128)S(1)} %get-tuple-element.2, s32[16]{0:T(128)S(1)} %select_reduce_fusion.2, s32[8]{0:T(128)S(1)} %select_reduce_fusion.3), dimensions={0} | concatenate | bytes 960 | tf_op jit(solution)/shard_map/concatenate | solution.py:232
  3.9 0.7 convert_rsqrt_fusion.1
  4.6 0.7 convert_rsqrt_fusion
  5.3 0.1 broadcast_in_dim.79.si
  5.4 0.2 broadcast_in_dim.78.su
  5.6 0.0 copy-start
  5.6 1.9 %copy-done = bf16[24,256,256]{2,1,0:T(8,128)(2,1)S(1)} copy-done((bf16[24,256,256]{2,1,0:T(8,128)(2,1)S(1)}, bf16[24,256,256]{2,1,0:T(8,128)(2,1)}, u32[]{:S(2)}) %copy-start) | copy-done | bytes 3145752
  7.5 0.0 copy-start.1
  7.5 0.9 %copy-done.1 = bf16[1024,128]{1,0:T(8,128)(2,1)S(1)} copy-done((bf16[1024,128]{1,0:T(8,128)(2,1)S(1)}, bf16[1024,128]{1,0:T(8,128)(2,1)}, u32[]{:S(2)}) %copy-start.1) | copy-done | bytes 262168
  8.4 0.0 copy-start.2
  8.4 0.9 %copy-done.2 = bf16[512,128]{1,0:T(8,128)(2,1)S(1)} copy-done((bf16[512,128]{1,0:T(8,128)(2,1)S(1)}, bf16[512,128]{1,0:T(8,128)(2,1)}, u32[]{:S(2)}) %copy-start.2) | copy-done | bytes 131096
  9.3 60.7 %shard_map.86 = (bf16[1024,128]{1,0:T(8,128)(2,1)S(1)}, bf16[512,128]{1,0:T(8,128)(2,1)S(1)}) custom-call(s32[120]{0:T(128)S(1)} %concatenate.3.idx, bf16[1024,128]{1,0:T(8,128)(2,1)S(1)} %copy-done.1, bf16[512,128]{1,0:T(8,128)(2,1)S(1)} %copy-done.2, f32[1024,128]{1,0:T(8,128)S(1)} %broadcast_in_dim.78.su, f32[512,128]{1,0:T(8,128)S(1)} %broadcast_in_dim.79.si, ...), custom_call_target="tpu_custom_call" | custom-call | tf_op jit(solution)/shard_map/pallas_call | solution.py:245
  70.0 0.7 copy.11
  70.7 0.7 copy.12
  (2 shorter events, 0.0 us)
Async XLA Ops:
  5.6 1.9 %copy-start = (bf16[24,256,256]{2,1,0:T(8,128)(2,1)S(1)}, bf16[24,256,256]{2,1,0:T(8,128)(2,1)}, u32[]{:S(2)}) copy-start(bf16[24,256,256]{2,1,0:T(8,128)(2,1)} %tiles_hbm.1) | copy-start | bytes 9437188
  7.5 0.9 %copy-start.1 = (bf16[1024,128]{1,0:T(8,128)(2,1)S(1)}, bf16[1024,128]{1,0:T(8,128)(2,1)}, u32[]{:S(2)}) copy-start(bf16[1024,128]{1,0:T(8,128)(2,1)} %gu.1) | copy-start | bytes 786436
  8.4 0.9 %copy-start.2 = (bf16[512,128]{1,0:T(8,128)(2,1)S(1)}, bf16[512,128]{1,0:T(8,128)(2,1)}, u32[]{:S(2)}) copy-start(bf16[512,128]{1,0:T(8,128)(2,1)} %gi.1) | copy-start | bytes 393220

commit v2 on v1

--- a/solution.py
+++ b/solution.py
@@ -54,58 +54,99 @@
     def slot(ref, l, d, rows):
         return ref.at[l, d] if rows % tile == 0 else ref.at[l, d, 0]
 
-    def gather_items(l, d):
-        return pltpu.make_async_remote_copy(
-            src_ref=part(items_all[l], mr, i_rows),
-            dst_ref=part(items_all[l], mr, i_rows),
-            send_sem=i_send.at[l, 0, d],
-            recv_sem=i_recv.at[l, 0, d],
-            device_id={"row": lax.rem(mr + d, n_row)},
-            device_id_type=MESH,
-        )
-
-    def gather_users(l, d):
-        return pltpu.make_async_remote_copy(
-            src_ref=part(users_all[l], mc, u_rows),
-            dst_ref=part(users_all[l], mc, u_rows),
-            send_sem=u_send.at[l, 0, d],
-            recv_sem=u_recv.at[l, 0, d],
-            device_id={"col": lax.rem(mc + d, n_col)},
-            device_id_type=MESH,
-        )
-
-    def scatter_items(l, d):
-        peer = lax.rem(mr + d, n_row)
-        return pltpu.make_async_remote_copy(
-            src_ref=part(ip_out.at[l], peer, i_rows),
-            dst_ref=slot(ip_in, l, d, i_rows),
-            send_sem=i_send.at[l, 1, d],
-            recv_sem=i_recv.at[l, 1, d],
-            device_id={"row": peer},
-            device_id_type=MESH,
-        )
-
-    def scatter_users(l, d):
-        peer = lax.rem(mc + d, n_col)
-        return pltpu.make_async_remote_copy(
-            src_ref=part(up_out.at[l], peer, u_rows),
-            dst_ref=slot(up_in, l, d, u_rows),
-            send_sem=u_send.at[l, 1, d],
-            recv_sem=u_recv.at[l, 1, d],
-            device_id={"col": peer},
-            device_id_type=MESH,
-        )
-
-    def each(copies, l, n, act):
-        def body(d, carry):
-            act(copies(l, d))
-            return carry
-
-        lax.fori_loop(1, n, body, 0)
-
-    start = lambda c: c.start()
-    wait_recv = lambda c: c.wait_recv()
-    wait_send = lambda c: c.wait_send()
+    def address(at, rows, chunk):
+        sub = min(rows, tile)
+        return lax.div(at, sub), pl.ds(pl.multiple_of(lax.rem(at, sub), chunk), chunk)
+
+    class Route:
+        def __init__(self, axis, me, n, rows, gathered, out, inn, send, recv):
+            self.n, self.rows, self.me, self.axis = n, rows, me, axis
+            self.gathered, self.out, self.inn, self.send, self.recv = gathered, out, inn, send, recv
+            self.relayed = n == 4
+            one = me + 1 - 2 * lax.rem(me, 2)
+            self.peer = (me, one, lax.rem(me + 2, 4), lax.rem(one + 2, 4))
+            self.terms = 3 if self.relayed else n
+
+        def remote(self, src, dst, l, kind, d, peer):
+            return pltpu.make_async_remote_copy(
+                src_ref=src,
+                dst_ref=dst,
+                send_sem=self.send.at[l, kind, d],
+                recv_sem=self.recv.at[l, kind, d],
+                device_id={self.axis: peer},
+                device_id_type=MESH,
+            )
+
+        def gather(self, l, d):
+            if self.relayed:
+                owner, to = self.peer[2 if d == 3 else 0], self.peer[2 if d == 2 else 1]
+            else:
+                owner, to = self.me, lax.rem(self.me + d, self.n)
+            at = part(self.gathered[l], owner, self.rows)
+            return self.remote(at, at, l, 0, d, to)
+
+        def scatter(self, l, d):
+            if self.relayed:
+                piece, to = self.peer[d], self.peer[2 if d == 2 else 1]
+            else:
+                piece = to = lax.rem(self.me + d, self.n)
+            return self.remote(
+                part(self.out.at[l], piece, self.rows), slot(self.inn, l, d, self.rows), l, 1, d, to
+            )
+
+        def each(self, copies, l, act, some):
+            if self.relayed:
+                for d in some:
+                    act(copies(l, d))
+            else:
+                def body(d, carry):
+                    act(copies(l, d))
+                    return carry
+
+                lax.fori_loop(1, self.n, body, 0)
+
+        def gather_start(self, l):
+            self.each(self.gather, l, lambda c: c.start(), (2, 1))
+
+        def gather_relay(self, l):
+            if self.relayed:
+                self.gather(l, 2).wait_recv()
+                self.gather(l, 3).start()
+
+        def gather_wait(self, l):
+            self.each(self.gather, l, lambda c: c.wait_recv(), (1, 3))
+
+        def scatter_start(self, l):
+            self.each(self.scatter, l, lambda c: c.start(), (3, 1))
+
+        def scatter_relay(self, l):
+            if self.relayed:
+                self.scatter(l, 3).wait_recv()
+                chunk = min(self.rows, 128)
+
+                def body(k, carry):
+                    at = self.peer[2] * self.rows + k * chunk
+                    block = lax.div(at, tile)
+                    mine = pl.ds(pl.multiple_of(lax.rem(at, tile), chunk), chunk)
+                    sub, there = address(k * chunk, self.rows, chunk)
+                    self.out[l, block, mine, :] = (
+                        self.out[l, block, mine, :].astype(jnp.float32)
+                        + self.inn[l, 3, sub, there, :].astype(jnp.float32)
+                    ).astype(jnp.bfloat16)
+                    return carry
+
+                lax.fori_loop(0, self.rows // chunk, body, 0)
+                self.scatter(l, 2).start()
+
+        def scatter_wait(self, l):
+            self.each(self.scatter, l, lambda c: c.wait_recv(), (1, 2))
+
+        def finish(self, l):
+            self.each(self.gather, l, lambda c: c.wait_send(), (1, 2, 3))
+            self.each(self.scatter, l, lambda c: c.wait_send(), (1, 2, 3))
+
+    items = Route("row", mr, n_row, i_rows, items_all, ip_out, ip_in, i_send, i_recv)
+    users = Route("col", mc, n_col, u_rows, users_all, up_out, up_in, u_send, u_recv)
 
     def begin(rows, own, grad, scale, gathered):
         chunk = min(rows, 128)
@@ -125,8 +166,8 @@
     begin(i_rows, mr * i_rows, gi, si, items_all)
     begin(u_rows, mc * u_rows, gu, su, users_all)
     pl.semaphore_wait(barrier, n_row + n_col - 2)
-    each(gather_items, 0, n_row, start)
-    each(gather_users, 0, n_col, start)
+    items.gather_start(0)
+    users.gather_start(0)
 
     sum_u[0] = jnp.zeros((tile, width), jnp.float32)
     sum_i[0] = jnp.zeros((tile, width), jnp.float32)
@@ -170,11 +211,10 @@
             block = lax.div(at, tile)
             mine = pl.ds(pl.multiple_of(lax.rem(at, tile), chunk), chunk)
             total = out[l, block, mine, :].astype(jnp.float32)
-            sub = min(rows, tile)
-            sub_at = pl.ds(pl.multiple_of(lax.rem(k * chunk, sub), chunk), chunk)
+            sub, there = address(k * chunk, rows, chunk)
 
             def add(d, total):
-                return total + inn[l, d, lax.div(k * chunk, sub), sub_at, :].astype(jnp.float32)
+                return total + inn[l, d, sub, there, :].astype(jnp.float32)
 
             if n <= 8:
                 for d in range(1, n):
@@ -192,27 +232,29 @@
         lax.fori_loop(0, rows // chunk, body, 0)
 
     for l in range(LAYERS):
-        each(gather_users, l, n_col, wait_recv)
+        users.gather_relay(l)
+        items.gather_relay(l)
+        users.gather_wait(l)
         products(l, tiles_t, users_all, sum_i, at_row, at_prev_col)
         stage(l, ip_out, sum_i, at_last_col, i_blocks)
-        each(scatter_items, l, n_row, start)
-        each(gather_items, l, n_row, wait_recv)
+        items.scatter_start(l)
+        items.gather_wait(l)
         products(l, tiles, items_all, sum_u, at_col, at_prev_row)
         stage(l, up_out, sum_u, at_last_row, u_blocks)
-        each(scatter_users, l, n_col, start)
-        each(scatter_items, l, n_row, wait_recv)
-        update(l, n_row, i_rows, mr * i_rows, gi, si, ip_out, ip_in, out_i, items_all)
+        users.scatter_start(l)
+        items.scatter_relay(l)
+        users.scatter_relay(l)
+        items.scatter_wait(l)
+        update(l, items.terms, i_rows, mr * i_rows, gi, si, ip_out, ip_in, out_i, items_all)
         if l + 1 < LAYERS:
-            each(gather_items, l + 1, n_row, start)
-        each(scatter_users, l, n_col, wait_recv)
-        update(l, n_col, u_rows, mc * u_rows, gu, su, up_out, up_in, out_u, users_all)
+            items.gather_start(l + 1)
+        users.scatter_wait(l)
+        update(l, users.terms, u_rows, mc * u_rows, gu, su, up_out, up_in, out_u, users_all)
         if l + 1 < LAYERS:
-            each(gather_users, l + 1, n_col, start)
+            users.gather_start(l + 1)
     for l in range(LAYERS):
-        each(gather_items, l, n_row, wait_send)
-        each(gather_users, l, n_col, wait_send)
-        each(scatter_items, l, n_row, wait_send)
-        each(scatter_users, l, n_col, wait_send)
+        items.finish(l)
+        users.finish(l)
 
 
 def shards(grad_users, grad_items, user_degree, item_degree, tile_values, tile_row, tile_col):

time: 71.7 us -> 63.8 us (0.89)
  the two profiles are of different devices: /device:TPU:9 before, /device:TPU:0 now
where the time goes in v2:
time: 63.8 us; the launch traced here: 63.5 us
  Pallas kernels  52.8 us (83%)
  local copies, waits for them, and re-layouts  6.17 us (10%)
  other arithmetic  3.86 us (6%)
  between operations  0.68 us (1%)
    pallas_call x1, Pallas kernels, shards(): pl.pallas_call(functools.partial(kernel, n_row, n_col, n_tiles, tile, wid...  52.8 us
    unnamed x8, local copies, waits for them, and re-layouts  5.1 us
    reduce_max x3, other arithmetic, latest(): return jnp.max(jnp.where(hit, slot[None, :] + 1, 0), axis=1)  2.47 us

profile of v2, /device:TPU:0, one launch (start us, length us, event | category | flops | bytes accessed | tf_op | source)
XLA Modules:
  0.0 63.5 jit_solution(9924539557013315693)
XLA Ops:
  0.7 0.8 %select_reduce_fusion.3 = s32[8]{0:T(128)S(1)} fusion(s32[24]{0:T(128)S(1)} %iota_add_fusion, s32[24]{0:T(128)} %param.13, pred[24]{0:T(512)(128)(4,1)S(1)} %iota_compare_fusion.3), kind=kLoop, calls=%fused_computation.9 | loop fusion | flops 760 | bytes 248 | tf_op jit(solution)/shard_map/reduce_max | solution.py:272
  1.4 0.8 %select_reduce_fusion.2 = s32[16]{0:T(128)S(1)} fusion(s32[24]{0:T(128)S(1)} %iota_add_fusion, s32[24]{0:T(128)} %param.12, pred[24]{0:T(512)(128)(4,1)S(1)} %iota_compare_fusion.3), kind=kLoop, calls=%fused_computation.5 | loop fusion | flops 1520 | bytes 280 | tf_op jit(solution)/shard_map/reduce_max | solution.py:272
  2.2 0.9 %select_reduce_fusion = (s32[24]{0:T(128)S(1)}, s32[24]{0:T(128)S(1)}) fusion(s32[24]{0:T(128)} %param.13, s32[24]{0:T(128)S(1)} %iota_add_fusion, s32[24]{0:T(128)} %param.12), kind=kLoop, calls=%fused_computation | loop fusion | flops 5136 | bytes 480 | tf_op jit(solution)/shard_map/reduce_max | solution.py:272
  3.1 0.8 %concatenate.3.idx = s32[120]{0:T(128)S(1)} concatenate(s32[24]{0:T(128)} %param.12, s32[24]{0:T(128)} %param.13, s32[24]{0:T(128)S(1)} %get-tuple-element.3, s32[24]{0:T(128)S(1)} %get-tuple-element.2, s32[16]{0:T(128)S(1)} %select_reduce_fusion.2, s32[8]{0:T(128)S(1)} %select_reduce_fusion.3), dimensions={0} | concatenate | bytes 960 | tf_op jit(solution)/shard_map/concatenate | solution.py:274
  3.9 0.7 %convert_rsqrt_fusion.1 = f32[512]{0:T(512)S(1)} fusion(s32[512]{0:T(512)} %param.10), kind=kLoop, calls=%fused_computation.12 | loop fusion | flops 512 | bytes 4096 | tf_op jit(solution)/shard_map/rsqrt | solution.py:267
  4.6 0.7 %convert_rsqrt_fusion = f32[1024]{0:T(1024)S(1)} fusion(s32[1024]{0:T(1024)} %param.9), kind=kLoop, calls=%fused_computation.8 | loop fusion | flops 1024 | bytes 8192 | tf_op jit(solution)/shard_map/rsqrt | solution.py:266
  5.3 0.1 broadcast_in_dim.79.si
  5.4 0.2 broadcast_in_dim.78.su
  5.6 0.0 copy-start
  5.6 1.9 %copy-done = bf16[24,256,256]{2,1,0:T(8,128)(2,1)S(1)} copy-done((bf16[24,256,256]{2,1,0:T(8,128)(2,1)S(1)}, bf16[24,256,256]{2,1,0:T(8,128)(2,1)}, u32[]{:S(2)}) %copy-start) | copy-done | bytes 3145752
  7.5 0.0 copy-start.1
  7.5 0.9 %copy-done.1 = bf16[1024,128]{1,0:T(8,128)(2,1)S(1)} copy-done((bf16[1024,128]{1,0:T(8,128)(2,1)S(1)}, bf16[1024,128]{1,0:T(8,128)(2,1)}, u32[]{:S(2)}) %copy-start.1) | copy-done | bytes 262168
  8.4 0.0 copy-start.2
  8.4 0.9 %copy-done.2 = bf16[512,128]{1,0:T(8,128)(2,1)S(1)} copy-done((bf16[512,128]{1,0:T(8,128)(2,1)S(1)}, bf16[512,128]{1,0:T(8,128)(2,1)}, u32[]{:S(2)}) %copy-start.2) | copy-done | bytes 131096
  9.3 52.8 %shard_map.86 = (bf16[1024,128]{1,0:T(8,128)(2,1)S(1)}, bf16[512,128]{1,0:T(8,128)(2,1)S(1)}) custom-call(s32[120]{0:T(128)S(1)} %concatenate.3.idx, bf16[1024,128]{1,0:T(8,128)(2,1)S(1)} %copy-done.1, bf16[512,128]{1,0:T(8,128)(2,1)S(1)} %copy-done.2, f32[1024,128]{1,0:T(8,128)S(1)} %broadcast_in_dim.78.su, f32[512,128]{1,0:T(8,128)S(1)} %broadcast_in_dim.79.si, ...), custom_call_target="tpu_custom_call" | custom-call | tf_op jit(solution)/shard_map/pallas_call | solution.py:287
  62.1 0.7 %copy.11 = bf16[1024,128]{1,0:T(8,128)(2,1)} copy(bf16[1024,128]{1,0:T(8,128)(2,1)S(1)} %get-tuple-element.6) | data formatting | bytes 524288
  62.8 0.7 %copy.12 = bf16[512,128]{1,0:T(8,128)(2,1)} copy(bf16[512,128]{1,0:T(8,128)(2,1)S(1)} %get-tuple-element.7) | data formatting | bytes 262144
  (2 shorter events, 0.0 us)
Async XLA Ops:
  5.6 1.9 %copy-start = (bf16[24,256,256]{2,1,0:T(8,128)(2,1)S(1)}, bf16[24,256,256]{2,1,0:T(8,128)(2,1)}, u32[]{:S(2)}) copy-start(bf16[24,256,256]{2,1,0:T(8,128)(2,1)} %tiles_hbm.1) | copy-start | bytes 9437188
  7.5 0.9 %copy-start.1 = (bf16[1024,128]{1,0:T(8,128)(2,1)S(1)}, bf16[1024,128]{1,0:T(8,128)(2,1)}, u32[]{:S(2)}) copy-start(bf16[1024,128]{1,0:T(8,128)(2,1)} %gu.1) | copy-start | bytes 786436
  8.4 0.9 %copy-start.2 = (bf16[512,128]{1,0:T(8,128)(2,1)S(1)}, bf16[512,128]{1,0:T(8,128)(2,1)}, u32[]{:S(2)}) copy-start(bf16[512,128]{1,0:T(8,128)(2,1)} %gi.1) | copy-start | bytes 393220

commit v3 on v2

--- a/solution.py
+++ b/solution.py
@@ -14,17 +14,15 @@
 
 def kernel(
     n_row, n_col, n_tiles, tile, width, u_rows, i_rows,
-    idx, gu, gi, su, si, tiles_hbm,
+    tile_row, tile_col, gu_hbm, gi_hbm, du_hbm, di_hbm, tiles_hbm,
     out_u, out_i,
     users_0, users_1, items_0, items_1, up_out, up_in, ip_out, ip_in, sum_u, sum_i, tiles, tiles_t,
-    u_send, u_recv, i_send, i_recv, tile_sem,
+    gu, gi, du, di, su, si, prev_row, prev_col, last_row, last_col,
+    u_send, u_recv, i_send, i_recv, load_sem,
 ):
     mr, mc = lax.axis_index("row"), lax.axis_index("col")
     u_blocks = u_rows * n_col // tile
     i_blocks = i_rows * n_row // tile
-    at_row, at_col = 0, n_tiles
-    at_prev_row, at_prev_col = 2 * n_tiles, 3 * n_tiles
-    at_last_row, at_last_col = 4 * n_tiles, 4 * n_tiles + u_blocks
 
     barrier = pltpu.get_barrier_semaphore()
 
@@ -39,8 +37,14 @@
 
     greet("row", mr, n_row)
     greet("col", mc, n_col)
-    tile_copy = pltpu.make_async_copy(tiles_hbm, tiles, tile_sem)
-    tile_copy.start()
+    loads = [
+        pltpu.make_async_copy(src, dst, load_sem.at[k])
+        for k, (src, dst) in enumerate(
+            ((di_hbm, di), (gi_hbm, gi), (du_hbm, du), (gu_hbm, gu), (tiles_hbm, tiles))
+        )
+    ]
+    for load in loads:
+        load.start()
 
     users_all, items_all = (users_0, users_1), (items_0, items_1)
 
@@ -163,15 +167,49 @@
 
         lax.fori_loop(0, rows // chunk, body, 0)
 
+    def scales(rows, degree, scale):
+        chunk = min(rows, 128)
+        for k in range(rows // chunk):
+            line = lax.rsqrt(degree[k : k + 1, :].astype(jnp.float32))
+            scale[k * chunk : (k + 1) * chunk, :] = jnp.broadcast_to(line, (width, chunk)).T
+
+    loads[0].wait()
+    scales(i_rows, di, si)
+    loads[1].wait()
     begin(i_rows, mr * i_rows, gi, si, items_all)
-    begin(u_rows, mc * u_rows, gu, su, users_all)
     pl.semaphore_wait(barrier, n_row + n_col - 2)
     items.gather_start(0)
+    loads[2].wait()
+    scales(u_rows, du, su)
+    loads[3].wait()
+    begin(u_rows, mc * u_rows, gu, su, users_all)
     users.gather_start(0)
+
+    def latest(keys, wanted, before):
+        found = jnp.int32(0)
+        for m in range(n_tiles):
+            found = jnp.where((keys[m] == wanted) & (m < before), m + 1, found)
+        return found
+
+    def previous(n, carry):
+        prev_row[n] = latest(tile_row, tile_row[n], n)
+        prev_col[n] = latest(tile_col, tile_col[n], n)
+        return carry
+
+    def last(keys, out):
+        def body(b, carry):
+            out[b] = latest(keys, b, n_tiles)
+            return carry
+
+        return body
+
+    lax.fori_loop(0, n_tiles, previous, 0)
+    lax.fori_loop(0, u_blocks, last(tile_row, last_row), 0)
+    lax.fori_loop(0, i_blocks, last(tile_col, last_col), 0)
 
     sum_u[0] = jnp.zeros((tile, width), jnp.float32)
     sum_i[0] = jnp.zeros((tile, width), jnp.float32)
-    tile_copy.wait()
+    loads[4].wait()
 
     def turn(n, carry):
         tiles_t[n] = tiles[n].T
@@ -181,23 +219,23 @@
 
     group = 4 if n_tiles % 4 == 0 else 1
 
-    def products(l, mats, blocks, sums, at_block, at_prev):
+    def products(l, mats, blocks, sums, block_of, prev):
         def body(g, carry):
             parts = []
             for k in range(group):
                 n = g * group + k
-                b = idx[at_block + n]
+                b = block_of[n]
                 parts.append(jnp.dot(mats[n], blocks[l][b], preferred_element_type=jnp.float32))
             for k in range(group):
                 n = g * group + k
-                sums[n + 1] = parts[k] + sums[idx[at_prev + n]]
+                sums[n + 1] = parts[k] + sums[prev[n]]
             return carry
 
         lax.fori_loop(0, n_tiles // group, body, 0)
 
-    def stage(l, out, sums, at_last, blocks):
+    def stage(l, out, sums, last, blocks):
         def body(b, carry):
-            out[l, b] = sums[idx[at_last + b]].astype(jnp.bfloat16)
+            out[l, b] = sums[last[b]].astype(jnp.bfloat16)
             return carry
 
         lax.fori_loop(0, blocks, body, 0)
@@ -235,12 +273,12 @@
         users.gather_relay(l)
         items.gather_relay(l)
         users.gather_wait(l)
-        products(l, tiles_t, users_all, sum_i, at_row, at_prev_col)
-        stage(l, ip_out, sum_i, at_last_col, i_blocks)
+        products(l, tiles_t, users_all, sum_i, tile_row, prev_col)
+        stage(l, ip_out, sum_i, last_col, i_blocks)
         items.scatter_start(l)
         items.gather_wait(l)
-        products(l, tiles, items_all, sum_u, at_col, at_prev_row)
-        stage(l, up_out, sum_u, at_last_row, u_blocks)
+        products(l, tiles, items_all, sum_u, tile_col, prev_row)
+        stage(l, up_out, sum_u, last_row, u_blocks)
         users.scatter_start(l)
         items.scatter_relay(l)
         users.scatter_relay(l)
@@ -263,24 +301,9 @@
     u_rows, width = grad_users.shape
     i_rows = grad_items.shape[0]
     u_blocks, i_blocks = u_rows * n_col // tile, i_rows * n_row // tile
-    su = jnp.broadcast_to(lax.rsqrt(user_degree.astype(jnp.float32))[:, None], (u_rows, width))
-    si = jnp.broadcast_to(lax.rsqrt(item_degree.astype(jnp.float32))[:, None], (i_rows, width))
-    slot = jnp.arange(n_tiles, dtype=jnp.int32)
-
-    def latest(keys, wanted, before):
-        hit = (keys[None, :] == wanted[:, None]) & (slot[None, :] < before[:, None])
-        return jnp.max(jnp.where(hit, slot[None, :] + 1, 0), axis=1)
-
-    idx = jnp.concatenate(
-        [
-            tile_row,
-            tile_col,
-            latest(tile_row, tile_row, slot),
-            latest(tile_col, tile_col, slot),
-            latest(tile_row, jnp.arange(u_blocks, dtype=jnp.int32), jnp.full(u_blocks, n_tiles)),
-            latest(tile_col, jnp.arange(i_blocks, dtype=jnp.int32), jnp.full(i_blocks, n_tiles)),
-        ]
-    )
+    u_chunk, i_chunk = min(u_rows, 128), min(i_rows, 128)
+    du = user_degree.reshape(u_rows // u_chunk, u_chunk)
+    di = item_degree.reshape(i_rows // i_chunk, i_chunk)
     u_sub, i_sub = min(u_rows, tile), min(i_rows, tile)
     vmem = pl.BlockSpec(memory_space=pltpu.VMEM)
     bf16, f32 = jnp.bfloat16, jnp.float32
@@ -290,8 +313,8 @@
             jax.ShapeDtypeStruct((u_rows, width), bf16),
             jax.ShapeDtypeStruct((i_rows, width), bf16),
         ),
-        in_specs=[pl.BlockSpec(memory_space=pltpu.SMEM), vmem, vmem, vmem, vmem,
-                  pl.BlockSpec(memory_space=pl.ANY)],
+        in_specs=[pl.BlockSpec(memory_space=pltpu.SMEM)] * 2
+        + [pl.BlockSpec(memory_space=pl.ANY)] * 5,
         out_specs=(vmem, vmem),
         scratch_shapes=[
             pltpu.VMEM((u_blocks, tile, width), bf16),
@@ -306,16 +329,26 @@
             pltpu.VMEM((n_tiles + 1, tile, width), f32),
             pltpu.VMEM((n_tiles, tile, tile), bf16),
             pltpu.VMEM((n_tiles, tile, tile), bf16),
+            pltpu.VMEM((u_rows, width), bf16),
+            pltpu.VMEM((i_rows, width), bf16),
+            pltpu.VMEM(du.shape, jnp.int32),
+            pltpu.VMEM(di.shape, jnp.int32),
+            pltpu.VMEM((u_rows, width), f32),
+            pltpu.VMEM((i_rows, width), f32),
+            pltpu.SMEM((n_tiles,), jnp.int32),
+            pltpu.SMEM((n_tiles,), jnp.int32),
+            pltpu.SMEM((u_blocks,), jnp.int32),
+            pltpu.SMEM((i_blocks,), jnp.int32),
             pltpu.SemaphoreType.DMA((LAYERS, 2, n_col)),
             pltpu.SemaphoreType.DMA((LAYERS, 2, n_col)),
             pltpu.SemaphoreType.DMA((LAYERS, 2, n_row)),
             pltpu.SemaphoreType.DMA((LAYERS, 2, n_row)),
-            pltpu.SemaphoreType.DMA,
+            pltpu.SemaphoreType.DMA((5,)),
         ],
         compiler_params=pltpu.CompilerParams(
-            collective_id=0, has_side_effects=True, vmem_limit_bytes=40 * 1024 * 1024
+            collective_id=0, has_side_effects=True, vmem_limit_bytes=56 * 1024 * 1024
         ),
-    )(idx, grad_users, grad_items, su, si, tile_values)
+    )(tile_row, tile_col, grad_users, grad_items, du, di, tile_values)
 
 
 def solution(mesh):

time: 63.8 us -> 57.9 us (0.908)
  other arithmetic: 3.86 us -> 0 us
  local copies, waits for them, and re-layouts: 6.17 us -> 3.24 us
  Pallas kernels: 52.8 us -> 53.8 us
    reduce_max x3 -> x0, other arithmetic: 2.47 us -> none  [latest(): return jnp.max(jnp.where(hit, slot[None, :] + 1, 0), axis=1)]
    unnamed x8 -> x2, local copies, waits for them, and re-layouts: 5.1 us -> 3.24 us
    rsqrt x2 -> x0, other arithmetic: 1.38 us -> none  [the longest x1 0.69 us: shards(): lax.rsqrt(user_degree.astype(jnp.float32))[:, None]]
    pallas_call x1, Pallas kernels: 52.8 us -> 53.8 us  [shards(): pl.pallas_call(functools.partial(kernel, n_row, n_col, n_tiles, tile, wid...]
    concatenate x1 -> x0, local copies, waits for them, and re-layouts: 0.75 us -> none  [shards(): jnp.concatenate([tile_row, tile_col, latest(tile_row, tile_row, slot), la...]
where the time goes in v3:
time: 57.9 us; the launch traced here: 57.7 us
  Pallas kernels  53.8 us (93%)
  local copies, waits for them, and re-layouts  3.24 us (6%)
  between operations  0.64 us (1%)
    pallas_call x1, Pallas kernels, shards(): pl.pallas_call(functools.partial(kernel, n_row, n_col, n_tiles, tile, wid...  53.8 us
    unnamed x2, local copies, waits for them, and re-layouts  3.24 us

profile of v3, /device:TPU:0, one launch (start us, length us, event | category | flops | bytes accessed | tf_op | source)
XLA Modules:
  0.0 57.7 jit_solution(11818633207699665511)
XLA Ops:
  0.6 53.8 %shard_map.86 = (bf16[1024,128]{1,0:T(8,128)(2,1)}, bf16[512,128]{1,0:T(8,128)(2,1)}) custom-call(s32[24]{0:T(128)} %tile_row.1, s32[24]{0:T(128)} %tile_col.1, bf16[1024,128]{1,0:T(8,128)(2,1)} %gu_hbm.1, bf16[512,128]{1,0:T(8,128)(2,1)} %gi_hbm.1, s32[8,128]{1,0:T(8,128)} %bitcast.2, s32[4,128]{1,0:T(4,128)} %bitcast.3, bf16[24,256,256]{2,1,0:T(8,128)(2,1)} %tiles_hbm.1), custom_call_target="tpu_custom_call" | custom-call | tf_op jit(solution)/shard_map/pallas_call | solution.py:310
  54.5 1.7 %copy.11 = bf16[1024,128]{1,0:T(8,128)(2,1)} copy(bf16[1024,128]{1,0:T(8,128)(2,1)} %get-tuple-element.4) | data formatting | bytes 524288
  56.2 1.6 %copy.12 = bf16[512,128]{1,0:T(8,128)(2,1)} copy(bf16[512,128]{1,0:T(8,128)(2,1)} %get-tuple-element.5) | data formatting | bytes 262144

commit v4 on v3

--- a/solution.py
+++ b/solution.py
@@ -121,7 +121,7 @@
             self.each(self.gather, l, lambda c: c.wait_recv(), (1, 3))
 
         def scatter_start(self, l):
-            self.each(self.scatter, l, lambda c: c.start(), (3, 1))
+            self.each(self.scatter, l, lambda c: c.start(), (3,))
 
         def scatter_relay(self, l):
             if self.relayed:
@@ -141,6 +141,7 @@
 
                 lax.fori_loop(0, self.rows // chunk, body, 0)
                 self.scatter(l, 2).start()
+                self.scatter(l, 1).start()
 
         def scatter_wait(self, l):
             self.each(self.scatter, l, lambda c: c.wait_recv(), (1, 2))
@@ -203,19 +204,14 @@
 
         return body
 
-    lax.fori_loop(0, n_tiles, previous, 0)
-    lax.fori_loop(0, u_blocks, last(tile_row, last_row), 0)
-    lax.fori_loop(0, i_blocks, last(tile_col, last_col), 0)
 
     sum_u[0] = jnp.zeros((tile, width), jnp.float32)
     sum_i[0] = jnp.zeros((tile, width), jnp.float32)
-    loads[4].wait()
 
     def turn(n, carry):
         tiles_t[n] = tiles[n].T
         return carry
 
-    lax.fori_loop(0, n_tiles, turn, 0)
 
     group = 4 if n_tiles % 4 == 0 else 1
 
@@ -272,6 +268,12 @@
     for l in range(LAYERS):
         users.gather_relay(l)
         items.gather_relay(l)
+        if l == 0:
+            loads[4].wait()
+            lax.fori_loop(0, n_tiles, previous, 0)
+            lax.fori_loop(0, u_blocks, last(tile_row, last_row), 0)
+            lax.fori_loop(0, i_blocks, last(tile_col, last_col), 0)
+            lax.fori_loop(0, n_tiles, turn, 0)
         users.gather_wait(l)
         products(l, tiles_t, users_all, sum_i, tile_row, prev_col)
         stage(l, ip_out, sum_i, last_col, i_blocks)

time: 57.9 us -> 56.6 us (0.978)
  Pallas kernels: 53.8 us -> 52.5 us
    pallas_call x1, Pallas kernels: 53.8 us -> 52.5 us  [shards(): pl.pallas_call(functools.partial(kernel, n_row, n_col, n_tiles, tile, wid...]
where the time goes in v4:
time: 56.6 us; the launch traced here: 56.4 us
  Pallas kernels  52.5 us (93%)
  local copies, waits for them, and re-layouts  3.24 us (6%)
  between operations  0.64 us (1%)
    pallas_call x1, Pallas kernels, shards(): pl.pallas_call(functools.partial(kernel, n_row, n_col, n_tiles, tile, wid...  52.5 us
    unnamed x2, local copies, waits for them, and re-layouts  3.24 us

profile of v4, /device:TPU:0, one launch (start us, length us, event | category | flops | bytes accessed | tf_op | source)
XLA Modules:
  0.0 56.4 jit_solution(13070540407256120441)
XLA Ops:
  0.6 52.5 %shard_map.86 = (bf16[1024,128]{1,0:T(8,128)(2,1)}, bf16[512,128]{1,0:T(8,128)(2,1)}) custom-call(s32[24]{0:T(128)} %tile_row.1, s32[24]{0:T(128)} %tile_col.1, bf16[1024,128]{1,0:T(8,128)(2,1)} %gu_hbm.1, bf16[512,128]{1,0:T(8,128)(2,1)} %gi_hbm.1, s32[8,128]{1,0:T(8,128)} %bitcast.2, s32[4,128]{1,0:T(4,128)} %bitcast.3, bf16[24,256,256]{2,1,0:T(8,128)(2,1)} %tiles_hbm.1), custom_call_target="tpu_custom_call" | custom-call | tf_op jit(solution)/shard_map/pallas_call | solution.py:312
  53.2 1.7 %copy.11 = bf16[1024,128]{1,0:T(8,128)(2,1)} copy(bf16[1024,128]{1,0:T(8,128)(2,1)} %get-tuple-element.4) | data formatting | bytes 524288
  54.8 1.6 %copy.12 = bf16[512,128]{1,0:T(8,128)(2,1)} copy(bf16[512,128]{1,0:T(8,128)(2,1)} %get-tuple-element.5) | data formatting | bytes 262144

commit v5 on v4

--- a/solution.py
+++ b/solution.py
@@ -67,11 +67,16 @@
             self.n, self.rows, self.me, self.axis = n, rows, me, axis
             self.gathered, self.out, self.inn, self.send, self.recv = gathered, out, inn, send, recv
             self.relayed = n == 4
+            self.halves = 2 if self.relayed and rows % (2 * tile) == 0 else 1
             one = me + 1 - 2 * lax.rem(me, 2)
             self.peer = (me, one, lax.rem(me + 2, 4), lax.rem(one + 2, 4))
             self.terms = 3 if self.relayed else n
 
-        def remote(self, src, dst, l, kind, d, peer):
+        def remote(self, src, dst, l, kind, d, h, peer):
+            if self.halves > 1:
+                k = self.rows // tile // self.halves
+                src, dst = src.at[pl.ds(h * k, k)], dst.at[pl.ds(h * k, k)]
+            d = h * self.n + d
             return pltpu.make_async_remote_copy(
                 src_ref=src,
                 dst_ref=dst,
@@ -81,27 +86,28 @@
                 device_id_type=MESH,
             )
 
-        def gather(self, l, d):
+        def gather(self, l, d, h=0):
             if self.relayed:
                 owner, to = self.peer[2 if d == 3 else 0], self.peer[2 if d == 2 else 1]
             else:
                 owner, to = self.me, lax.rem(self.me + d, self.n)
             at = part(self.gathered[l], owner, self.rows)
-            return self.remote(at, at, l, 0, d, to)
-
-        def scatter(self, l, d):
+            return self.remote(at, at, l, 0, d, h, to)
+
+        def scatter(self, l, d, h=0):
             if self.relayed:
                 piece, to = self.peer[d], self.peer[2 if d == 2 else 1]
             else:
                 piece = to = lax.rem(self.me + d, self.n)
             return self.remote(
-                part(self.out.at[l], piece, self.rows), slot(self.inn, l, d, self.rows), l, 1, d, to
+                part(self.out.at[l], piece, self.rows), slot(self.inn, l, d, self.rows), l, 1, d, h, to
             )
 
         def each(self, copies, l, act, some):
             if self.relayed:
                 for d in some:
-                    act(copies(l, d))
+                    for h in range(self.halves):
+                        act(copies(l, d, h))
             else:
                 def body(d, carry):
                     act(copies(l, d))
@@ -114,8 +120,9 @@
 
         def gather_relay(self, l):
             if self.relayed:
-                self.gather(l, 2).wait_recv()
-                self.gather(l, 3).start()
+                for h in range(self.halves):
+                    self.gather(l, 2, h).wait_recv()
+                    self.gather(l, 3, h).start()
 
         def gather_wait(self, l):
             self.each(self.gather, l, lambda c: c.wait_recv(), (1, 3))
@@ -125,7 +132,6 @@
 
         def scatter_relay(self, l):
             if self.relayed:
-                self.scatter(l, 3).wait_recv()
                 chunk = min(self.rows, 128)
 
                 def body(k, carry):
@@ -139,9 +145,13 @@
                     ).astype(jnp.bfloat16)
                     return carry
 
-                lax.fori_loop(0, self.rows // chunk, body, 0)
-                self.scatter(l, 2).start()
-                self.scatter(l, 1).start()
+                count = self.rows // chunk // self.halves
+                for h in range(self.halves):
+                    self.scatter(l, 3, h).wait_recv()
+                    lax.fori_loop(h * count, (h + 1) * count, body, 0)
+                    self.scatter(l, 2, h).start()
+                for h in range(self.halves):
+                    self.scatter(l, 1, h).start()
 
         def scatter_wait(self, l):
             self.each(self.scatter, l, lambda c: c.wait_recv(), (1, 2))
@@ -213,7 +223,7 @@
         return carry
 
 
-    group = 4 if n_tiles % 4 == 0 else 1
+    group = 8 if n_tiles % 8 == 0 else 1
 
     def products(l, mats, blocks, sums, block_of, prev):
         def body(g, carry):
@@ -341,10 +351,10 @@
             pltpu.SMEM((n_tiles,), jnp.int32),
             pltpu.SMEM((u_blocks,), jnp.int32),
             pltpu.SMEM((i_blocks,), jnp.int32),
-            pltpu.SemaphoreType.DMA((LAYERS, 2, n_col)),
-            pltpu.SemaphoreType.DMA((LAYERS, 2, n_col)),
-            pltpu.SemaphoreType.DMA((LAYERS, 2, n_row)),
-            pltpu.SemaphoreType.DMA((LAYERS, 2, n_row)),
+            pltpu.SemaphoreType.DMA((LAYERS, 2, 2 * n_col)),
+            pltpu.SemaphoreType.DMA((LAYERS, 2, 2 * n_col)),
+            pltpu.SemaphoreType.DMA((LAYERS, 2, 2 * n_row)),
+            pltpu.SemaphoreType.DMA((LAYERS, 2, 2 * n_row)),
             pltpu.SemaphoreType.DMA((5,)),
         ],
         compiler_params=pltpu.CompilerParams(

time: 56.6 us -> 54.3 us (0.959)
  Pallas kernels: 52.5 us -> 50.2 us
    pallas_call x1, Pallas kernels: 52.5 us -> 50.2 us  [shards(): pl.pallas_call(functools.partial(kernel, n_row, n_col, n_tiles, tile, wid...]
where the time goes in v5:
time: 54.3 us; the launch traced here: 54.1 us
  Pallas kernels  50.2 us (92%)
  local copies, waits for them, and re-layouts  3.24 us (6%)
  between operations  0.64 us (1%)
    pallas_call x1, Pallas kernels, shards(): pl.pallas_call(functools.partial(kernel, n_row, n_col, n_tiles, tile, wid...  50.2 us
    unnamed x2, local copies, waits for them, and re-layouts  3.24 us

profile of v5, /device:TPU:0, one launch (start us, length us, event | category | flops | bytes accessed | tf_op | source)
XLA Modules:
  0.0 54.1 jit_solution(10386229113740685001)
XLA Ops:
  0.6 50.2 %shard_map.86 = (bf16[1024,128]{1,0:T(8,128)(2,1)}, bf16[512,128]{1,0:T(8,128)(2,1)}) custom-call(s32[24]{0:T(128)} %tile_row.1, s32[24]{0:T(128)} %tile_col.1, bf16[1024,128]{1,0:T(8,128)(2,1)} %gu_hbm.1, bf16[512,128]{1,0:T(8,128)(2,1)} %gi_hbm.1, s32[8,128]{1,0:T(8,128)} %bitcast.2, s32[4,128]{1,0:T(4,128)} %bitcast.3, bf16[24,256,256]{2,1,0:T(8,128)(2,1)} %tiles_hbm.1), custom_call_target="tpu_custom_call" | custom-call | tf_op jit(solution)/shard_map/pallas_call | solution.py:322
  50.9 1.7 %copy.11 = bf16[1024,128]{1,0:T(8,128)(2,1)} copy(bf16[1024,128]{1,0:T(8,128)(2,1)} %get-tuple-element.4) | data formatting | bytes 524288
  52.5 1.6 %copy.12 = bf16[512,128]{1,0:T(8,128)(2,1)} copy(bf16[512,128]{1,0:T(8,128)(2,1)} %get-tuple-element.5) | data formatting | bytes 262144
